TPU v7x, 128 devices: a whole 4x4x4 slice. The times are simulated.
128 devices in a mesh: tok: 8 (over z, core), lat: 16 (over y, x).
Axes of the slice: x: 4, y: 4, z: 4, core: 2. Of those that a mesh axis runs over, the one named last changes fastest.
Arguments:
- activations: bfloat16 [2048, 2, 8192], P('lat', None, 'tok'), may hold values from -6 to 6
- enc_weight: bfloat16 [64, 2, 8192, 256], P('lat', None, 'tok'), may hold values from -0.046875 to 0.046875
- enc_bias: float32 [64, 256], P('lat'), may hold values from -3 to 3
- dec_weight: bfloat16 [64, 256, 2, 8192], P('lat', None, None, 'tok'), may hold values from -0.09375 to 0.09375
- dec_bias: float32 [2, 8192], P(None, 'tok'), may hold values from -3 to 3
- active: int32 [16, 16], replicated, may hold values from 0 to 63, all different within a row; in each aligned block of 16 rows (0 to 15, 16 to 31, ...) at most 8 rows name the same one
Outputs:
- grad_enc: bfloat16 [64, 2, 8192, 256], P('lat', None, 'tok')
- grad_enc_bias: float32 [64, 256], P('lat')
- grad_dec: bfloat16 [64, 256, 2, 8192], P('lat', None, None, 'tok')
- grad_dec_bias: float32 [2, 8192], P(None, 'tok')
Inputs may be any that keep to these rules, and one draw needn't show every extreme that they name: `active`: each row lists 16 different block ids; every block id appears in some row; no block id appears in more than 8 rows, and some block id appears in exactly 8 rows.
All inputs are finite; a program needn't handle non-finite values.
Results may differ from a plain program's by a relative error of at most 0.02.
Values may be sent and summed in bfloat16 or wider, within the bound.
A program may use at most 192 MiB of HBM per device.

v0:
```python
import math
import jax
import jax.numpy as jnp
from jax import lax
from jax.sharding import PartitionSpec as P

MOST = 8
TILE = 128
SPARSITY = 0.25
NORM_EPSILON = 1e-06


def slot_lists(active, first_block, block_count):
    tile_count = active.shape[0]
    block_ids = first_block + jnp.arange(block_count, dtype=jnp.int32)
    is_active = jnp.any(active[:, :, None] == block_ids[None, None, :], axis=1).astype(jnp.int32)
    rank_count = jnp.cumsum(is_active, axis=0)
    wanted = jnp.arange(MOST, dtype=jnp.int32) + 1
    picked = (is_active[:, :, None] == 1) & (rank_count[:, :, None] == wanted[None, None, :])
    tile_ids = jnp.arange(tile_count, dtype=jnp.int32)
    slot_tile = jnp.sum(jnp.where(picked, tile_ids[:, None, None], 0), axis=0)
    live_slot = jnp.any(picked, axis=0)
    return (slot_tile, live_slot)


def on_device(activations, enc_weight, enc_bias, dec_weight, dec_bias, active):
    slab_count = enc_weight.shape[0]
    tile_count = active.shape[0]
    tile_rows = activations.shape[0]
    models = activations.shape[1]
    feat_width = activations.shape[2]
    loss_scale = 1.0 / math.sqrt(MOST * TILE)
    first_block = lax.axis_index("lat") * slab_count
    slot_tile, live_slot = slot_lists(active, first_block, slab_count)
    live_mask = live_slot[:, :, None, None]
    gathered = lax.all_gather(activations, "lat", axis=0, tiled=True)
    tile_acts = gathered.reshape(tile_count, tile_rows, models, feat_width)
    chosen = tile_acts[slot_tile]
    pre_part = jnp.einsum(
        "smrad,sadj->smrj", chosen, enc_weight, preferred_element_type=jnp.float32
    )
    pre_act = lax.psum(pre_part, "tok") + enc_bias[:, None, None, :]
    features = jnp.where(live_mask, jnp.maximum(pre_act, 0.0), 0.0).astype(jnp.bfloat16)
    product = jnp.einsum(
        "smrj,sjad->smrad", features, dec_weight, preferred_element_type=jnp.float32
    )
    partial_value = (
        jnp.zeros((tile_count, tile_rows, models, feat_width), jnp.float32)
        .at[slot_tile]
        .add(product)
    )
    rounded = lax.optimization_barrier(partial_value.astype(jnp.bfloat16)).astype(jnp.float32)
    rounded = rounded.reshape(tile_count * tile_rows, models, feat_width)
    recon_mine = (
        lax.psum_scatter(
            rounded.astype(jnp.bfloat16), "lat", scatter_dimension=0, tiled=True
        ).astype(jnp.float32)
        + dec_bias[None, :, :]
    )
    error_mine = (recon_mine - activations.astype(jnp.float32)).astype(jnp.bfloat16)
    error_all = lax.all_gather(error_mine, "lat", axis=0, tiled=True)
    tile_err = error_all.reshape(tile_count, tile_rows, models, feat_width)
    err_chosen = tile_err[slot_tile]
    grad_part = jnp.einsum(
        "smrad,sjad->smrj", err_chosen, dec_weight, preferred_element_type=jnp.float32
    )
    dec_wide = dec_weight.astype(jnp.float32)
    squares = jnp.sum(jnp.square(dec_wide), axis=3)
    grad_sum, square_sum = (
        lax.psum(grad_part.astype(jnp.bfloat16), "tok").astype(jnp.float32),
        lax.psum(squares.astype(jnp.bfloat16), "tok").astype(jnp.float32),
    )
    dec_norms = jnp.sqrt(square_sum + NORM_EPSILON)
    feat_grad = loss_scale * (grad_sum + SPARSITY * jnp.sum(dec_norms, axis=2)[:, None, None, :])
    pre_grad = jnp.where(features > 0, feat_grad, 0.0).astype(jnp.bfloat16)
    grad_enc = jnp.einsum(
        "smrad,smrj->sadj", chosen, pre_grad, preferred_element_type=jnp.float32
    ).astype(jnp.bfloat16)
    grad_enc_bias = jnp.sum(pre_grad.astype(jnp.float32), axis=(1, 2))
    feat_total = jnp.sum(features.astype(jnp.float32), axis=(1, 2))
    recon_term = jnp.einsum(
        "smrj,smrad->sjad", features, err_chosen, preferred_element_type=jnp.float32
    )
    norm_term = SPARSITY * feat_total[:, :, None, None] * dec_wide / dec_norms[:, :, :, None]
    grad_dec = (loss_scale * (recon_term + norm_term)).astype(jnp.bfloat16)
    grad_dec_bias = loss_scale * jnp.sum(error_all.astype(jnp.float32), axis=0)
    return (grad_enc, grad_enc_bias, grad_dec, grad_dec_bias)


def solution(mesh):
    placed = (
        P("lat", None, "tok"),
        P("lat", None, "tok", None),
        P("lat", None),
        P("lat", None, None, "tok"),
        P(None, "tok"),
        P(),
    )
    return jax.shard_map(
        on_device,
        mesh=mesh,
        in_specs=placed,
        out_specs=(
            P("lat", None, "tok", None),
            P("lat", None),
            P("lat", None, None, "tok"),
            P(None, "tok"),
        ),
        check_vma=False,
    )
```

profile of v0, /device:TPU:0, one launch (start us, length us, event | category | flops | bytes accessed | tf_op | source)
XLA Modules:
  0.0 585.7 jit_solution(5982257089558291725)
XLA Ops:
  7.2 0.0 all-gather.3.cloned.1.call-start
  7.2 2.0 copy.46
  9.2 0.0 all-gather.3.cloned.1.call-update
  9.2 0.0 all-reduce.3.cloned.1.call-start
  9.3 0.9 compare_reduce_fusion
  10.2 0.1 copy.47
  10.3 0.1 copy.48
  10.4 0.2 select_reduce_fusion
  10.6 0.1 reshape.64
  10.7 73.1 %all-gather.3.cloned.1.call-done = bf16[2048,2,1024]{2,0,1:T(8,128)(2,1)} async-done(((bf16[128,2,1024]{2,0,1:T(8,128)(2,1)}), bf16[2048,2,1024]{2,0,1:T(8,128)(2,1)}) %all-gather.3.cloned.1.call-update) | async-done | bytes 8388624 | tf_op jit(solution)/shard_map/all_gather | solution.py:36
  83.8 8.2 %copy.49 = bf16[16,128,2,1024]{3,1,2,0:T(8,128)(2,1)} copy(bf16[16,128,2,1024]{3,1,0,2:T(8,128)(2,1)} %bitcast.69) | data formatting | bytes 16777216 | tf_op jit(solution)/shard_map/reshape | solution.py:37
  92.0 10.6 %gather_fusion = bf16[32,128,2,1024]{3,1,2,0:T(8,128)(2,1)} fusion(bf16[16,128,2,1024]{3,1,2,0:T(8,128)(2,1)} %copy.49, s32[1024]{0:T(1024)S(1)} %pad_clamp_fusion), kind=kCustom, calls=%fused_computation | custom fusion | bytes 33554560 | tf_op jit(solution)/shard_map/gather | solution.py:38
  102.6 13.5 %fusion.11 = f32[4,8,128,256]{3,2,1,0:T(8,128)} fusion(bf16[4,8,128,2,1024]{4,2,3,1,0:T(8,128)(2,1)} %bitcast.65, bf16[4,2,1024,256]{3,2,1,0:T(8,128)(2,1)} %param.7), kind=kOutput, calls=%fused_computation.23 | convolution fusion | flops 4294967296 | bytes 25165824 | tf_op jit(solution)/shard_map/smrad,sadj->smrj/dot_general | solution.py:39
  116.1 0.0 copy-start.4
  116.1 0.0 all-reduce.3.cloned.1.call-update
  116.1 0.2 reduce-scatter.2.cloned.1.call-start
  116.4 0.2 fusion.19
  116.6 72.3 %all-reduce.3.cloned.1.call-done = f32[4,8,128,256]{3,2,1,0:T(8,128)} async-done(((f32[4,8,128,256]{3,2,1,0:T(8,128)}), f32[4,8,128,256]{3,2,1,0:T(8,128)}) %all-reduce.3.cloned.1.call-update) | async-done | bytes 4194320 | tf_op jit(solution)/shard_map/psum | solution.py:42
  188.9 0.0 copy-done.4
  188.9 0.0 copy-start
  188.9 3.1 select_convert_fusion.1
  192.0 0.4 copy-done
  192.3 13.1 %fusion.9 = f32[4,8,128,2,1024]{4,2,3,1,0:T(8,128)} fusion(bf16[4,256,2,1024,1]{3,2,1,0,4:T(2,128)(2,1)S(1)} %bitcast.64, bf16[4,8,128,256]{3,2,1,0:T(8,128)(2,1)S(1)} %select_convert_fusion.1), kind=kOutput, calls=%fused_computation.21 | convolution fusion | flops 4294967296 | bytes 39845888 | tf_op jit(solution)/shard_map/smrj,sjad->smrad/dot_general | solution.py:44
  205.4 7.8 %broadcast_in_dim.28 = f32[16,128,2,1024]{3,1,2,0:T(8,128)} broadcast(f32[]{:T(128)} %constant.17.clone.1), dimensions={} | broadcast | bytes 16777220 | tf_op jit(solution)/shard_map/broadcast_in_dim | solution.py:48
  213.3 65.6 %scatter_fusion = f32[16,128,2,1024]{3,1,2,0:T(8,128)} fusion(f32[16,128,2,1024]{3,1,2,0:T(8,128)} %broadcast_in_dim.28, s32[32]{0:T(128)S(1)} %reshape.64, f32[32,128,2,1024]{3,1,2,0:T(8,128)} %bitcast.60), kind=kCustom, calls=%fused_computation.2 | custom fusion | flops 8388608 | bytes 100663424 | tf_op jit(solution)/shard_map/scatter-add | solution.py:50
  278.9 9.1 %convert_element_type.66 = bf16[16,128,2,1024]{3,1,2,0:T(8,128)(2,1)} convert(f32[16,128,2,1024]{3,1,2,0:T(8,128)} %scatter_fusion) | non-fusion elementwise | flops 4194304 | bytes 25165824 | tf_op jit(solution)/shard_map/convert_element_type | solution.py:52
  288.0 8.2 %copy.51 = bf16[16,128,2,1024]{3,1,0,2:T(8,128)(2,1)} copy(bf16[16,128,2,1024]{3,1,2,0:T(8,128)(2,1)} %convert_element_type.66) | data formatting | bytes 16777216 | tf_op jit(solution)/shard_map/optimization_barrier | solution.py:52
  296.2 0.0 copy-start.3
  296.2 0.0 copy-start.5
  296.2 0.0 reduce-scatter.2.cloned.1.call-update
  296.2 0.0 all-gather.5.cloned.1.call-start
  296.2 84.8 %reduce-scatter.2.cloned.1.call-done = bf16[128,2,1024]{2,0,1:T(8,128)(2,1)} async-done(((bf16[2048,2,1024]{2,0,1:T(8,128)(2,1)}), bf16[128,2,1024]{2,0,1:T(8,128)(2,1)}) %reduce-scatter.2.cloned.1.call-update) | async-done | bytes 524304 | tf_op jit(solution)/shard_map/reduce_scatter | solution.py:55
  381.1 0.0 copy-done.3
  381.1 0.0 copy-done.5
  381.1 2.1 subtract_convert_fusion
  383.1 0.0 all-gather.5.cloned.1.call-update
  383.2 0.0 all-reduce.5.cloned.1.call-start
  383.2 3.4 fusion
  386.6 13.9 %psum.23 = bf16[4,256,2]{1,2,0:T(2,128)(2,1)S(1)} all-reduce(bf16[4,256,2]{1,2,0:T(2,128)(2,1)S(1)} %fusion), channel_id=1, replica_groups=mesh['tok'=8,'lat'=16] {'tok'}, use_global_device_ids=true, to_apply=%region_9.10 | all-reduce | flops 2048 | bytes 8192 | tf_op jit(solution)/shard_map/psum | solution.py:71
  400.5 53.2 %all-gather.5.cloned.1.call-done = bf16[2048,2,1024]{2,0,1:T(8,128)(2,1)} async-done(((bf16[128,2,1024]{2,0,1:T(8,128)(2,1)}), bf16[2048,2,1024]{2,0,1:T(8,128)(2,1)}) %all-gather.5.cloned.1.call-update) | async-done | bytes 8388624 | tf_op jit(solution)/shard_map/all_gather | solution.py:61
  453.7 10.6 %gather_fusion.1 = bf16[32,128,2,1024]{3,1,2,0:T(8,128)(2,1)} fusion(bf16[16,128,2,1024]{3,1,0,2:T(8,128)(2,1)} %bitcast.61, s32[1024]{0:T(1024)S(1)} %pad_clamp_fusion), kind=kCustom, calls=%fused_computation.1 | custom fusion | bytes 33554560 | tf_op jit(solution)/shard_map/gather | solution.py:63
  464.4 12.8 %bitcast_convert_fusion.1 = bf16[4,8,128,256]{3,2,1,0:T(8,128)(2,1)} fusion(bf16[4,8,128,2,1024]{4,2,3,1,0:T(8,128)(2,1)} %bitcast.67, bf16[4,256,2,1024,1]{3,2,1,0,4:T(2,128)(2,1)} %bitcast.63), kind=kOutput, calls=%fused_computation.14 | convolution fusion | flops 4296015872 | bytes 23068672 | tf_op jit(solution)/shard_map/smrad,sjad->smrj/dot_general | solution.py:64
  477.2 0.0 all-reduce.5.cloned.1.call-update
  477.3 5.0 convert_reduce_fusion
  482.3 0.6 broadcast_multiply_fusion
  482.9 60.1 %all-reduce.5.cloned.1.call-done = bf16[4,8,128,256]{3,2,1,0:T(8,128)(2,1)} async-done(((bf16[4,8,128,256]{3,2,1,0:T(8,128)(2,1)}), bf16[4,8,128,256]{3,2,1,0:T(8,128)(2,1)}) %all-reduce.5.cloned.1.call-update) | async-done | bytes 2097168 | tf_op jit(solution)/shard_map/psum | solution.py:70
  543.0 0.0 copy-start.1
  543.0 5.1 convert_reduce_fusion.1
  548.0 0.0 copy-done.1
  548.0 10.7 %fusion.4 = bf16[4,256,2,1024]{3,1,2,0:T(8,128)(2,1)} fusion(f32[4,256,2]{1,2,0:T(2,128)S(1)} %get-tuple-element.26, f32[4,256]{1,0:T(4,128)S(1)} %broadcast_multiply_fusion.1, bf16[4,256,2,1024]{3,2,1,0:T(2,128)(2,1)S(1)} %copy-done.1, bf16[4,8,128,2,1024]{4,2,3,1,0:T(8,128)(2,1)} %bitcast.68, bf16[4,8,128,256]{3,2,1,0:T(8,128)(2,1)S(1)} %select_convert_fusion.1), kind=kOutput, calls=%fused_computation.11 | convolution fusion | flops 4307550208 | bytes 27275264 | tf_op jit(solution)/shard_map/smrj,smrad->sjad/dot_general | solution.py:81
  558.7 0.0 copy-start.2
  558.7 8.7 %copy.58 = bf16[4,256,2,1024]{3,2,1,0:T(2,128)(2,1)} copy(bf16[4,256,2,1024]{3,1,2,0:T(8,128)(2,1)} %fusion.4) | data formatting | bytes 8388608
  567.4 0.0 copy-done.2
  567.4 11.8 %bitcast_convert_fusion = bf16[4,2,1024,256]{3,2,1,0:T(8,128)(2,1)} fusion(bf16[4,8,128,2,1024]{4,2,3,1,0:T(8,128)(2,1)} %bitcast.66, bf16[4,8,128,256]{3,2,1,0:T(8,128)(2,1)S(1)} %copy-done.2, bf16[4,8,128,256]{3,2,1,0:T(8,128)(2,1)S(1)} %select_convert_fusion.1, f32[4,256]{1,0:T(4,128)S(1)} %broadcast_multiply_fusion.2), kind=kOutput, calls=%fused_computation.10 | convolution fusion | flops 4303355904 | bytes 25169920 | tf_op jit(solution)/shard_map/smrad,smrj->sadj/dot_general | solution.py:76
  (9 shorter events, 0.1 us)
Async XLA Ops:
  7.2 76.7 %all-gather.3.cloned.1.call-start = ((), (), s32[]{:S(2)}) async-start(), calls=%async_computation.1 | async-start | bytes 8912896 | tf_op jit(solution)/shard_map/all_gather | solution.py:36
  9.2 179.7 %all-reduce.3.cloned.1.call-start = ((), (), s32[]{:S(2)}) async-start(), calls=%async_computation.2 | async-start | bytes 8388608 | tf_op jit(solution)/shard_map/psum | solution.py:42
  116.1 72.8 %copy-start.4 = (f32[4,256]{1,0:T(4,128)S(1)}, f32[4,256]{1,0:T(4,128)}, u32[]{:S(2)}) copy-start(f32[4,256]{1,0:T(4,128)} %param.8) | copy-start | bytes 12292
  116.1 265.0 %reduce-scatter.2.cloned.1.call-start = ((), (), s32[]{:S(2)}) async-start(), calls=%async_computation.3 | async-start | bytes 8912896 | tf_op jit(solution)/shard_map/reduce_scatter | solution.py:55
  188.9 3.4 copy-start
  296.2 84.9 %copy-start.3 = (bf16[128,2,1024]{2,1,0:T(2,128)(2,1)S(1)}, bf16[128,2,1024]{2,1,0:T(2,128)(2,1)}, u32[]{:S(2)}) copy-start(bf16[128,2,1024]{2,1,0:T(2,128)(2,1)} %param.6) | copy-start | bytes 1572868
  296.2 84.9 %copy-start.5 = (f32[2,1024]{1,0:T(2,128)S(1)}, f32[2,1024]{1,0:T(2,128)}, u32[]{:S(2)}) copy-start(f32[2,1024]{1,0:T(2,128)} %param.10) | copy-start | bytes 24580
  296.2 157.5 %all-gather.5.cloned.1.call-start = ((), (), s32[]{:S(2)}) async-start(), calls=%async_computation.4 | async-start | bytes 8912896 | tf_op jit(solution)/shard_map/all_gather | solution.py:61
  383.2 159.8 %all-reduce.5.cloned.1.call-start = ((), (), s32[]{:S(2)}) async-start(), calls=%async_computation.5 | async-start | bytes 4194304 | tf_op jit(solution)/shard_map/psum | solution.py:70
  543.0 5.1 copy-start.1
  558.7 8.7 %copy-start.2 = (bf16[4,8,128,256]{3,2,1,0:T(8,128)(2,1)S(1)}, bf16[4,8,128,256]{3,2,1,0:T(8,128)(2,1)}, u32[]{:S(2)}) copy-start(bf16[4,8,128,256]{3,2,1,0:T(8,128)(2,1)} %all-reduce.5.cloned.1.call-done) | copy-start | bytes 6291460
Sparse Core Ops, SparseCore 0:
  10.7 73.0 all-gather.2
  116.2 72.5 all-reduce.2
  296.3 84.7 reduce-scatter.1
  383.7 70.0 all-gather.4
  477.3 65.6 all-reduce.4
where the time goes:
time: 586 us
  waiting for transfers between devices  344 us (59%)
  other arithmetic  95.3 us (16%)
  matrix products  61.8 us (11%)
  local copies, waits for them, and re-layouts  56.7 us (10%)
  blocking collectives  13.9 us (2%)
  between operations  13.8 us (2%)
    reduce_scatter x1, waiting for transfers between devices, on_device(): lax.psum_scatter(rounded.astype(jnp.bfloat16), 'lat', scatter_dimension=0...  84.8 us
    all_gather x1, waiting for transfers between devices, on_device(): gathered = lax.all_gather(activations, 'lat', axis=0, tiled=True)  73.1 us
    psum x1, waiting for transfers between devices, on_device(): pre_act = lax.psum(pre_part, 'tok') + enc_bias[:, None, None, :]  72.3 us
    scatter-add x1, other arithmetic, on_device(): partial_value = jnp.zeros((tile_count, tile_rows, models, feat_width), jn...  65.6 us
    psum x1, waiting for transfers between devices, on_device(): lax.psum(grad_part.astype(jnp.bfloat16), 'tok').astype(jnp.float32)  60.1 us
    all_gather x1, waiting for transfers between devices, on_device(): error_all = lax.all_gather(error_mine, 'lat', axis=0, tiled=True)  53.2 us
    psum x1, blocking collectives, on_device(): lax.psum(squares.astype(jnp.bfloat16), 'tok').astype(jnp.float32)  13.9 us
    dot_general x1, matrix products, on_device(): jnp.einsum('smrad,sadj->smrj', chosen, enc_weight, preferred_element_type...  13.5 us
  transfers between devices with their start and end apart: 5, of which 5 were waited for; matrix products, arithmetic and copies ran while one was open for 2% of the time, Pallas kernels for 0%

commit v1 on v0

--- a/solution.py
+++ b/solution.py
@@ -39,7 +39,7 @@
     pre_part = jnp.einsum(
         "smrad,sadj->smrj", chosen, enc_weight, preferred_element_type=jnp.float32
     )
-    pre_act = lax.psum(pre_part, "tok") + enc_bias[:, None, None, :]
+    pre_act = jnp.sum(lax.all_gather(pre_part, "tok"), axis=0) + enc_bias[:, None, None, :]
     features = jnp.where(live_mask, jnp.maximum(pre_act, 0.0), 0.0).astype(jnp.bfloat16)
     product = jnp.einsum(
         "smrj,sjad->smrad", features, dec_weight, preferred_element_type=jnp.float32

time: 586 us -> 685 us (1.17)
  waiting for transfers between devices: 344 us -> 428 us
  other arithmetic: 95.3 us -> 110 us
    all_gather x0 -> x1, waiting for transfers between devices: none -> 155 us  [on_device(): lax.all_gather(pre_part, 'tok')]
    psum x1 -> x0, waiting for transfers between devices: 72.3 us -> none  [on_device(): pre_act = lax.psum(pre_part, 'tok') + enc_bias[:, None, None, :]]
    reduce_sum x0 -> x1, other arithmetic: none -> 14.3 us  [on_device(): jnp.sum(lax.all_gather(pre_part, 'tok'), axis=0)]
where the time goes in v1:
time: 685 us; the launch traced here: 684 us
  waiting for transfers between devices  428 us (62%)
  other arithmetic  110 us (16%)
  matrix products  61.8 us (9%)
  local copies, waits for them, and re-layouts  56.7 us (8%)
  blocking collectives  13.8 us (2%)
  between operations  13.8 us (2%)
    all_gather x1, waiting for transfers between devices, on_device(): lax.all_gather(pre_part, 'tok')  155 us
    reduce_scatter x1, waiting for transfers between devices, on_device(): lax.psum_scatter(rounded.astype(jnp.bfloat16), 'lat', scatter_dimension=0...  85.6 us
    all_gather x1, waiting for transfers between devices, on_device(): gathered = lax.all_gather(activations, 'lat', axis=0, tiled=True)  73.1 us
    scatter-add x1, other arithmetic, on_device(): partial_value = jnp.zeros((tile_count, tile_rows, models, feat_width), jn...  65.6 us
    psum x1, waiting for transfers between devices, on_device(): lax.psum(grad_part.astype(jnp.bfloat16), 'tok').astype(jnp.float32)  60.1 us
    all_gather x1, waiting for transfers between devices, on_device(): error_all = lax.all_gather(error_mine, 'lat', axis=0, tiled=True)  53.3 us
    reduce_sum x1, other arithmetic, on_device(): jnp.sum(lax.all_gather(pre_part, 'tok'), axis=0)  14.3 us
    psum x1, blocking collectives, on_device(): lax.psum(squares.astype(jnp.bfloat16), 'tok').astype(jnp.float32)  13.8 us
  transfers between devices with their start and end apart: 5, of which 5 were waited for; matrix products, arithmetic and copies ran while one was open for 2% of the time, Pallas kernels for 0%

profile of v1, /device:TPU:0, one launch (start us, length us, event | category | flops | bytes accessed | tf_op | source)
XLA Modules:
  0.0 684.0 jit_solution(8817741879537722139)
XLA Ops:
  7.2 0.0 all-gather.5.cloned.1.call-start
  7.2 2.0 copy.57
  9.2 0.0 all-gather.5.cloned.1.call-update
  9.2 0.0 all-gather.9.cloned.1.call-start
  9.3 0.9 compare_reduce_fusion
  10.2 0.1 copy.58
  10.3 0.1 copy.59
  10.4 0.2 select_reduce_fusion
  10.6 0.1 reshape.64
  10.7 73.1 %all-gather.5.cloned.1.call-done = bf16[2048,2,1024]{2,0,1:T(8,128)(2,1)} async-done(((bf16[128,2,1024]{2,0,1:T(8,128)(2,1)}), bf16[2048,2,1024]{2,0,1:T(8,128)(2,1)}) %all-gather.5.cloned.1.call-update) | async-done | bytes 8388624 | tf_op jit(solution)/shard_map/all_gather | solution.py:36
  83.8 8.2 %copy.60 = bf16[16,128,2,1024]{3,1,2,0:T(8,128)(2,1)} copy(bf16[16,128,2,1024]{3,1,0,2:T(8,128)(2,1)} %bitcast.71) | data formatting | bytes 16777216 | tf_op jit(solution)/shard_map/reshape | solution.py:37
  92.0 10.6 %gather_fusion = bf16[32,128,2,1024]{3,1,2,0:T(8,128)(2,1)} fusion(bf16[16,128,2,1024]{3,1,2,0:T(8,128)(2,1)} %copy.60, s32[1024]{0:T(1024)S(1)} %pad_clamp_fusion), kind=kCustom, calls=%fused_computation | custom fusion | bytes 33554560 | tf_op jit(solution)/shard_map/gather | solution.py:38
  102.6 13.5 %fusion.11 = f32[4,8,128,256]{3,2,1,0:T(8,128)} fusion(bf16[4,8,128,2,1024]{4,2,3,1,0:T(8,128)(2,1)} %bitcast.67, bf16[4,2,1024,256]{3,2,1,0:T(8,128)(2,1)} %param.7), kind=kOutput, calls=%fused_computation.23 | convolution fusion | flops 4294967296 | bytes 25165824 | tf_op jit(solution)/shard_map/smrad,sadj->smrj/dot_general | solution.py:39
  116.1 0.0 all-gather.9.cloned.1.call-update
  116.1 0.2 reduce-scatter.2.cloned.1.call-start
  116.4 0.2 fusion.19
  116.6 155.4 %all-gather.9.cloned.1.call-done = f32[32,8,128,256]{3,2,1,0:T(8,128)} async-done(((f32[4,8,128,256]{3,2,1,0:T(8,128)}), f32[32,8,128,256]{3,2,1,0:T(8,128)}) %all-gather.9.cloned.1.call-update) | async-done | bytes 33554448 | tf_op jit(solution)/shard_map/all_gather | solution.py:42
  272.0 0.0 copy-start.4
  272.0 14.3 %reduce_sum.67 = f32[4,8,128,256]{3,2,1,0:T(8,128)} reduce(f32[8,4,8,128,256]{4,3,2,1,0:T(8,128)} %bitcast.63, f32[]{:T(128)} %constant.17.clone.1), dimensions={0}, to_apply=%region_4.5 | reduce | flops 7340032 | bytes 37748740 | tf_op jit(solution)/shard_map/reduce_sum | solution.py:42
  286.3 0.0 copy-done.4
  286.3 0.0 copy-start
  286.3 3.1 select_convert_fusion.1
  289.4 0.4 copy-done
  289.8 13.1 %fusion.9 = f32[4,8,128,2,1024]{4,2,3,1,0:T(8,128)} fusion(bf16[4,256,2,1024,1]{3,2,1,0,4:T(2,128)(2,1)S(1)} %bitcast.66, bf16[4,8,128,256]{3,2,1,0:T(8,128)(2,1)S(1)} %select_convert_fusion.1), kind=kOutput, calls=%fused_computation.21 | convolution fusion | flops 4294967296 | bytes 39845888 | tf_op jit(solution)/shard_map/smrj,sjad->smrad/dot_general | solution.py:44
  302.9 7.8 %broadcast_in_dim.28 = f32[16,128,2,1024]{3,1,2,0:T(8,128)} broadcast(f32[]{:T(128)} %constant.17.clone.1), dimensions={} | broadcast | bytes 16777220 | tf_op jit(solution)/shard_map/broadcast_in_dim | solution.py:48
  310.8 65.6 %scatter_fusion = f32[16,128,2,1024]{3,1,2,0:T(8,128)} fusion(f32[16,128,2,1024]{3,1,2,0:T(8,128)} %broadcast_in_dim.28, s32[32]{0:T(128)S(1)} %reshape.64, f32[32,128,2,1024]{3,1,2,0:T(8,128)} %bitcast.61), kind=kCustom, calls=%fused_computation.2 | custom fusion | flops 8388608 | bytes 100663424 | tf_op jit(solution)/shard_map/scatter-add | solution.py:50
  376.4 9.1 %convert_element_type.66 = bf16[16,128,2,1024]{3,1,2,0:T(8,128)(2,1)} convert(f32[16,128,2,1024]{3,1,2,0:T(8,128)} %scatter_fusion) | non-fusion elementwise | flops 4194304 | bytes 25165824 | tf_op jit(solution)/shard_map/convert_element_type | solution.py:52
  385.5 8.2 %copy.62 = bf16[16,128,2,1024]{3,1,0,2:T(8,128)(2,1)} copy(bf16[16,128,2,1024]{3,1,2,0:T(8,128)(2,1)} %convert_element_type.66) | data formatting | bytes 16777216 | tf_op jit(solution)/shard_map/optimization_barrier | solution.py:52
  393.6 0.0 copy-start.3
  393.6 0.0 copy-start.5
  393.6 0.0 reduce-scatter.2.cloned.1.call-update
  393.7 0.0 all-gather.7.cloned.1.call-start
  393.7 85.6 %reduce-scatter.2.cloned.1.call-done = bf16[128,2,1024]{2,0,1:T(8,128)(2,1)} async-done(((bf16[2048,2,1024]{2,0,1:T(8,128)(2,1)}), bf16[128,2,1024]{2,0,1:T(8,128)(2,1)}) %reduce-scatter.2.cloned.1.call-update) | async-done | bytes 524304 | tf_op jit(solution)/shard_map/reduce_scatter | solution.py:55
  479.4 0.0 copy-done.3
  479.4 0.0 copy-done.5
  479.4 2.1 subtract_convert_fusion
  481.4 0.0 all-gather.7.cloned.1.call-update
  481.5 0.0 all-reduce.2.cloned.1.call-start
  481.5 3.4 fusion
  484.9 13.8 %psum.15 = bf16[4,256,2]{1,2,0:T(2,128)(2,1)S(1)} all-reduce(bf16[4,256,2]{1,2,0:T(2,128)(2,1)S(1)} %fusion), channel_id=1, replica_groups=mesh['tok'=8,'lat'=16] {'tok'}, use_global_device_ids=true, to_apply=%region_9.10 | all-reduce | flops 2048 | bytes 8192 | tf_op jit(solution)/shard_map/psum | solution.py:71
  498.7 53.3 %all-gather.7.cloned.1.call-done = bf16[2048,2,1024]{2,0,1:T(8,128)(2,1)} async-done(((bf16[128,2,1024]{2,0,1:T(8,128)(2,1)}), bf16[2048,2,1024]{2,0,1:T(8,128)(2,1)}) %all-gather.7.cloned.1.call-update) | async-done | bytes 8388624 | tf_op jit(solution)/shard_map/all_gather | solution.py:61
  552.0 10.6 %gather_fusion.1 = bf16[32,128,2,1024]{3,1,2,0:T(8,128)(2,1)} fusion(bf16[16,128,2,1024]{3,1,0,2:T(8,128)(2,1)} %bitcast.62, s32[1024]{0:T(1024)S(1)} %pad_clamp_fusion), kind=kCustom, calls=%fused_computation.1 | custom fusion | bytes 33554560 | tf_op jit(solution)/shard_map/gather | solution.py:63
  562.6 12.8 %bitcast_convert_fusion.1 = bf16[4,8,128,256]{3,2,1,0:T(8,128)(2,1)} fusion(bf16[4,8,128,2,1024]{4,2,3,1,0:T(8,128)(2,1)} %bitcast.69, bf16[4,256,2,1024,1]{3,2,1,0,4:T(2,128)(2,1)} %bitcast.65), kind=kOutput, calls=%fused_computation.14 | convolution fusion | flops 4296015872 | bytes 23068672 | tf_op jit(solution)/shard_map/smrad,sjad->smrj/dot_general | solution.py:64
  575.4 0.0 all-reduce.2.cloned.1.call-update
  575.5 5.0 convert_reduce_fusion
  580.5 0.6 broadcast_multiply_fusion
  581.1 60.1 %all-reduce.2.cloned.1.call-done = bf16[4,8,128,256]{3,2,1,0:T(8,128)(2,1)} async-done(((bf16[4,8,128,256]{3,2,1,0:T(8,128)(2,1)}), bf16[4,8,128,256]{3,2,1,0:T(8,128)(2,1)}) %all-reduce.2.cloned.1.call-update) | async-done | bytes 2097168 | tf_op jit(solution)/shard_map/psum | solution.py:70
  641.2 0.0 copy-start.1
  641.2 5.1 convert_reduce_fusion.1
  646.3 0.0 copy-done.1
  646.3 10.7 %fusion.4 = bf16[4,256,2,1024]{3,1,2,0:T(8,128)(2,1)} fusion(f32[4,256,2]{1,2,0:T(2,128)S(1)} %get-tuple-element.30, f32[4,256]{1,0:T(4,128)S(1)} %broadcast_multiply_fusion.1, bf16[4,256,2,1024]{3,2,1,0:T(2,128)(2,1)S(1)} %copy-done.1, bf16[4,8,128,2,1024]{4,2,3,1,0:T(8,128)(2,1)} %bitcast.70, bf16[4,8,128,256]{3,2,1,0:T(8,128)(2,1)S(1)} %select_convert_fusion.1), kind=kOutput, calls=%fused_computation.11 | convolution fusion | flops 4307550208 | bytes 27275264 | tf_op jit(solution)/shard_map/smrj,smrad->sjad/dot_general | solution.py:81
  657.0 0.0 copy-start.2
  657.0 8.7 %copy.69 = bf16[4,256,2,1024]{3,2,1,0:T(2,128)(2,1)} copy(bf16[4,256,2,1024]{3,1,2,0:T(8,128)(2,1)} %fusion.4) | data formatting | bytes 8388608
  665.6 0.0 copy-done.2
  665.7 11.8 %bitcast_convert_fusion = bf16[4,2,1024,256]{3,2,1,0:T(8,128)(2,1)} fusion(bf16[4,8,128,2,1024]{4,2,3,1,0:T(8,128)(2,1)} %bitcast.68, bf16[4,8,128,256]{3,2,1,0:T(8,128)(2,1)S(1)} %copy-done.2, bf16[4,8,128,256]{3,2,1,0:T(8,128)(2,1)S(1)} %select_convert_fusion.1, f32[4,256]{1,0:T(4,128)S(1)} %broadcast_multiply_fusion.2), kind=kOutput, calls=%fused_computation.10 | convolution fusion | flops 4303355904 | bytes 25169920 | tf_op jit(solution)/shard_map/smrad,smrj->sadj/dot_general | solution.py:76
  (9 shorter events, 0.1 us)
Async XLA Ops:
  7.2 76.7 %all-gather.5.cloned.1.call-start = ((), (), s32[]{:S(2)}) async-start(), calls=%async_computation.1 | async-start | bytes 8912896 | tf_op jit(solution)/shard_map/all_gather | solution.py:36
  9.2 262.8 %all-gather.9.cloned.1.call-start = ((), (), s32[]{:S(2)}) async-start(), calls=%async_computation.5 | async-start | bytes 37748736 | tf_op jit(solution)/shard_map/all_gather | solution.py:42
  116.1 363.2 %reduce-scatter.2.cloned.1.call-start = ((), (), s32[]{:S(2)}) async-start(), calls=%async_computation.2 | async-start | bytes 8912896 | tf_op jit(solution)/shard_map/reduce_scatter | solution.py:55
  272.0 14.4 %copy-start.4 = (f32[4,256]{1,0:T(4,128)S(1)}, f32[4,256]{1,0:T(4,128)}, u32[]{:S(2)}) copy-start(f32[4,256]{1,0:T(4,128)} %param.8) | copy-start | bytes 12292
  286.3 3.4 copy-start
  393.6 85.7 %copy-start.3 = (bf16[128,2,1024]{2,1,0:T(2,128)(2,1)S(1)}, bf16[128,2,1024]{2,1,0:T(2,128)(2,1)}, u32[]{:S(2)}) copy-start(bf16[128,2,1024]{2,1,0:T(2,128)(2,1)} %param.6) | copy-start | bytes 1572868
  393.6 85.7 %copy-start.5 = (f32[2,1024]{1,0:T(2,128)S(1)}, f32[2,1024]{1,0:T(2,128)}, u32[]{:S(2)}) copy-start(f32[2,1024]{1,0:T(2,128)} %param.10) | copy-start | bytes 24580
  393.7 158.3 %all-gather.7.cloned.1.call-start = ((), (), s32[]{:S(2)}) async-start(), calls=%async_computation.3 | async-start | bytes 8912896 | tf_op jit(solution)/shard_map/all_gather | solution.py:61
  481.5 159.8 %all-reduce.2.cloned.1.call-start = ((), (), s32[]{:S(2)}) async-start(), calls=%async_computation.4 | async-start | bytes 4194304 | tf_op jit(solution)/shard_map/psum | solution.py:70
  641.2 5.1 copy-start.1
  657.0 8.7 %copy-start.2 = (bf16[4,8,128,256]{3,2,1,0:T(8,128)(2,1)S(1)}, bf16[4,8,128,256]{3,2,1,0:T(8,128)(2,1)}, u32[]{:S(2)}) copy-start(bf16[4,8,128,256]{3,2,1,0:T(8,128)(2,1)} %all-reduce.2.cloned.1.call-done) | copy-start | bytes 6291460
Sparse Core Ops, SparseCore 0:
  10.7 73.0 all-gather.4
  116.2 155.6 all-gather.8
  393.8 85.5 reduce-scatter.1
  481.9 69.9 all-gather.6
  575.6 65.6 all-reduce.1
